TPU v7x, 256 devices: a whole 4x4x8 slice. The times are simulated.
256 devices in a mesh: band: 64 (over z_lo, y, x), dom: 4 (over z_hi, core).
Axes of the slice: x: 4, y: 4, z: 8 (z_hi: 2, z_lo: 4; z = z_hi * 4 + z_lo), core: 2. Of those that a mesh axis runs over, the one named last changes fastest.
Arguments:
- orbitals: float32 [128, 128, 16, 128], P('band', 'dom'), may hold values from -6 to 6
- potential: float32 [128, 16, 128], P('dom'), may hold values from -1 to 0
- subspace: float32 [128, 128], P('band'), may hold values from -0.4 to 2.4, as said below
Outputs:
- rotated: float32 [128, 262144], P(None, ('dom', 'band'))
Inputs may be any that keep to these rules, and one draw needn't show every extreme that they name: `subspace`: diagonal entries between 0.7 and 2.3, off-diagonal entries small and independent.
All inputs are finite; a program needn't handle non-finite values.
Results may differ from a plain program's by a relative error of at most 0.00012.
Values sent between devices are 32-bit elements; how exact they have to be, the bound alone decides.
A program may use at most 128 MiB of HBM per device.

v0:
```python
import functools
import math

import jax
import jax.numpy as jnp
from jax import lax
from jax.experimental import pallas as pl
from jax.experimental.pallas import tpu as pltpu
from jax.sharding import PartitionSpec as P

DEG = 3
REACH = 6
MESH = pl.DeviceIdType.MESH

upper_edge = 10.7
lower_edge = 1.5
bottom_edge = -1.0


def stencil_weights():
    factor_square = math.factorial(6) ** 2
    side_weights = []
    for offset in range(1, 7):
        side_weights.append(
            2.0
            * (-1.0) ** (offset + 1)
            * factor_square
            / (offset * offset * math.factorial(6 - offset) * math.factorial(6 + offset))
        )
    center_weight = -2.0 * sum(side_weights)
    return (center_weight, side_weights)


def filter_scalars(pass_count):
    half_width = (upper_edge - lower_edge) / 2.0
    sigma_now = half_width / (bottom_edge - (upper_edge + lower_edge) / 2.0)
    gamma_value = 2.0 / sigma_now
    scalars = [(sigma_now / half_width, 0.0)]
    for pass_index in range(pass_count - 1):
        sigma_next = 1.0 / (gamma_value - sigma_now)
        scalars.append((2.0 * sigma_next / half_width, sigma_now * sigma_next))
        sigma_now = sigma_next
    return scalars


def two_parts(values):
    high = values.astype(jnp.bfloat16)
    return high, (values - high.astype(jnp.float32)).astype(jnp.bfloat16)


def stencil_matrix(period, axis):
    rows = lax.broadcasted_iota(jnp.int32, (128, 128), 0)
    columns = lax.broadcasted_iota(jnp.int32, (128, 128), 1)
    apart = jnp.abs(rows - columns)
    if period < 128:
        same = jnp.bitwise_or(rows, period - 1) == jnp.bitwise_or(columns, period - 1)
        apart = jnp.where(same, apart, 0)
    apart = jnp.minimum(apart, period - apart)
    matrix = jnp.zeros((128, 128), jnp.float32)
    for k, w in enumerate(stencil_weights()[1], 1):
        matrix = jnp.where(apart == k, jnp.float32(w), matrix)
    high, low = two_parts(matrix)
    return jnp.concatenate([high, high, low], axis=axis)


def filtered_block(window, pot, before, scale, weight, lanes, rows):
    center_weight, side = stencil_weights()
    n = window.shape[0] - 2 * REACH
    mid = window[REACH : REACH + n]
    high, low = two_parts(mid.reshape(n * 16, 128))
    total = jnp.dot(
        jnp.concatenate([high, low, high], axis=1), lanes, preferred_element_type=jnp.float32
    ) + jnp.dot(
        rows, jnp.concatenate([high, low, high], axis=0), preferred_element_type=jnp.float32
    )
    total = total.reshape(n, 2, 8, 128)
    for k in range(1, REACH + 1):
        beside = window[REACH + k : REACH + k + n] + window[REACH - k : REACH - k + n]
        total = total + side[k - 1] * beside
    diag = (-1.5 * center_weight - (upper_edge + lower_edge) / 2.0) * scale
    result = (pot * scale + diag) * mid + (-0.5 * scale) * total
    if before is not None:
        result = result - weight * before
    return result


def filter_kernel(
    bands, orb, pot, sub, recv, rows, p0, p1, p2, out, pot_v,
    near_send, near_recv, far_send, far_recv, pot_send, pot_recv, pass_send, pass_recv,
    move_sem, all_send, all_recv, row_send, row_recv, plane_sem, all_sem,
):
    quarter = orb.shape[1]
    slab, whole = 2 * quarter, 4 * quarter
    band, dom = lax.axis_index("band"), lax.axis_index("dom")
    core, half = lax.rem(dom, 2), lax.div(dom, 2)
    side = 4
    floor = side * side
    zl, x, yx = lax.div(band, floor), lax.rem(band, side), lax.rem(band, floor)
    shift = 2 * REACH
    left = jnp.where(zl < side // 2, 1, 0)
    long = core == left
    base = half * slab
    own_tile = dom * bands + band
    own_plane = lax.div(own_tile, 2)
    scalars = filter_scalars(DEG)
    buffers = (p0, p1, p2)
    rims = tuple(shift + REACH * (DEG - level) for level in range(DEG + 1))
    pot_rim = rims[1]

    def placed(u, count):
        return jnp.where(left == 1, u, slab - count - u)

    load = pltpu.make_async_copy(
        orb.at[core], p0.at[pl.ds(core * quarter + rims[0], quarter)], move_sem.at[0]
    )
    load.start()
    load_pot = pltpu.make_async_copy(
        pot, pot_v.at[pl.ds(core * quarter + pot_rim, quarter)], move_sem.at[1]
    )
    load_pot.start()

    sibling = {"dom": dom + 1 - 2 * core}
    partners = [{"dom": 2 * (1 - half) + k} for k in range(2)]

    def chip_along(shift):
        there = lax.rem(half * side + zl + shift, 2 * side)
        return {
            "band": lax.rem(there, side) * floor + yx,
            "dom": lax.div(there, side) * 2 + core,
        }

    x_line = [
        {"band": band - x + lax.rem(x + dx, side), "dom": dom if dk == 0 else dom + 1 - 2 * core}
        for dx in range(side)
        for dk in range(2)
    ][1:]
    y = lax.div(yx, side)
    y_line = [{"band": band + side * (lax.rem(y + dy, side) - y)} for dy in range(1, side)]
    z_line = [chip_along(dz) for dz in range(1, 2 * side)]
    other_partner = {"dom": 2 * (1 - half) + 1 - core}
    barrier = pltpu.get_barrier_semaphore()
    entered = (*z_line, other_partner, *x_line, *y_line)

    def tell(peers, semaphore):
        for peer in peers:
            pl.semaphore_signal(semaphore, inc=1, device_id=peer, device_id_type=MESH)

    tell(entered, barrier)
    lanes, lines = stencil_matrix(128, 0), stencil_matrix(16, 1)
    pl.semaphore_wait(barrier, len(entered))

    def remote(src, dst, send_sem, recv_sem, peer):
        return pltpu.make_async_remote_copy(
            src_ref=src, dst_ref=dst, send_sem=send_sem, recv_sem=recv_sem,
            device_id=peer, device_id_type=MESH,
        )

    pieces = [(0, REACH)] + [(REACH + 8 * i, 8) for i in range(3)]
    assert sum(n for _, n in pieces) == rims[0]
    far = []
    for o in range(2):
        group = []
        for at, (a, n) in enumerate(pieces):
            group.append(
                remote(
                    orb.at[o, pl.ds(jnp.where(left == 1, quarter - a - n, a), n)],
                    p0.at[pl.ds(placed(-a - n, n) + rims[0], n)],
                    far_send.at[o, at], far_recv.at[at], partners[o],
                )
            )
        n = REACH
        group.append(
            remote(
                orb.at[o, pl.ds(jnp.where(left == 1, 0, quarter - n), n)],
                p0.at[pl.ds(placed(slab, n) + rims[0], n)],
                far_send.at[o, 4], far_recv.at[4], partners[o],
            )
        )
        far.append(group)
    part = pot_rim // 8
    pot_far = [
        remote(
            pot.at[pl.ds(jnp.where(left == 1, quarter - pot_rim, 0) + (2 * x + o) * part, part)],
            pot_v.at[pl.ds(placed(-pot_rim, pot_rim) + pot_rim + (2 * x + o) * part, part)],
            pot_send.at[o], pot_recv, partners[o],
        )
        for o in range(2)
    ]
    mine = pot_v.at[pl.ds(placed(-pot_rim, pot_rim) + pot_rim + (2 * x + core) * part, part)]

    @pl.when(long)
    def _():
        for o in range(2):
            pot_far[o].start()
        for o in range(2):
            far[o][0].start()

    @pl.when(jnp.logical_not(long))
    def _():
        for o in range(2):
            far[o][4].start()

    near = remote(
        orb.at[1 - core], p0.at[pl.ds(core * quarter + rims[0], quarter)],
        near_send.at[0], near_recv.at[0], sibling,
    )
    near_pot = remote(
        pot, pot_v.at[pl.ds(core * quarter + pot_rim, quarter)],
        near_send.at[1], near_recv.at[1], sibling,
    )
    near.start()
    near_pot.start()

    @pl.when(long)
    def _():
        for at in range(1, 4):
            for o in range(2):
                far[o][at].start()

    tell(y_line, plane_sem)

    step = 8

    def apply(level, u, blocks):
        scale, weight = scalars[level]

        def body(i, c):
            at = placed(u + i * step, step)
            before = None
            if level > 0:
                before = buffers[level - 1][pl.ds(at + rims[level - 1], step)]
            window = buffers[level][pl.ds(at + rims[level] - REACH, step + 2 * REACH)]
            pairs = filtered_block(
                window, pot_v[pl.ds(at + pot_rim, step)], before, scale, weight, lanes, lines
            )
            if level < DEG - 1:
                buffers[level + 1][pl.ds(at + rims[level + 1], step)] = pairs
            else:
                out[pl.ds(2 * (at + rims[DEG]), 2 * step)] = pairs.reshape(2 * step, 8, 128)
            return c

        lax.fori_loop(0, blocks, body, 0)

    row = 2 * band + core

    def spread(u, count):
        start = placed(u, count)
        tiles = 2 * count

        def send(i, c):
            at = lax.rem(i + yx * (tiles // floor), tiles)
            tile = lax.rem(2 * (base + start) + at + 2 * whole, 2 * whole)
            src = out.at[2 * (start + rims[DEG]) + at]

            @pl.when(tile != own_tile)
            def _():
                peer = {"band": lax.rem(tile, bands), "dom": lax.div(tile, bands)}
                remote(src, recv.at[row], all_send, all_recv, peer).start()

            @pl.when(tile == own_tile)
            def _():
                pltpu.make_async_copy(src, recv.at[row], move_sem.at[3]).start()

            return c

        lax.fori_loop(0, tiles, send, 0)

    def advance(u):
        for level in range(DEG):
            apply(level, u + level * REACH, 1)
        spread(u + (DEG - 1) * REACH, 8)

    load.wait()
    load_pot.wait()
    near.wait_recv()
    near_pot.wait_recv()
    pl.semaphore_wait(plane_sem, len(y_line))
    tell(z_line, all_sem)
    apply(0, 8, 6)
    apply(1, 14, 4)
    apply(1, 42, 1)
    apply(2, 20, 3)
    pl.semaphore_wait(all_sem, len(z_line))

    def send_rows(i, c):
        at = lax.rem(i + band, bands)
        plane = core * quarter + lax.div(at, 2)
        plane = jnp.where(
            left == 1,
            jnp.where(plane >= slab - shift, plane - slab, plane),
            jnp.where(plane < shift, plane + slab, plane),
        )
        tile = lax.rem(2 * (base + plane) + lax.rem(at, 2) + 2 * whole, 2 * whole)

        @pl.when(tile != own_tile)
        def _():
            peer = {"band": lax.rem(tile, bands), "dom": lax.div(tile, bands)}
            remote(sub, rows.at[band], row_send, row_recv, peer).start()

        return c

    lax.fori_loop(0, bands, send_rows, 0)
    own_rows = pltpu.make_async_copy(sub, rows.at[band], move_sem.at[2])
    own_rows.start()
    spread(20, 24)

    pot_far[0].wait_recv()
    passed = [
        remote(mine, mine, pass_send.at[at], pass_recv.at[at], peer)
        for at, peer in enumerate(x_line)
    ]
    for copy in passed:
        copy.start()

    far[0][4].wait_recv()
    apply(0, slab - 8, 1)
    apply(1, slab - 14, 1)
    apply(2, slab - 20, 1)
    spread(slab - 20, 8)
    for at in range(4):
        if at == 1:
            for copy in passed:
                copy.wait_recv()
        far[0][at].wait_recv()
        advance(-8 * at)

    @pl.when(long)
    def _():
        for o in range(2):
            pot_far[o].wait_send()
            for at in range(4):
                far[o][at].wait_send()

    @pl.when(jnp.logical_not(long))
    def _():
        for o in range(2):
            far[o][4].wait_send()

    for copy in (near, near_pot, *passed):
        copy.wait_send()
    own_rows.wait()
    pltpu.make_async_copy(out.at[0], recv.at[row], move_sem.at[3]).wait()
    for ref, sem_a, sem_b in ((rows, row_send, row_recv), (recv, all_send, all_recv)):
        all_but_own = ref.at[pl.ds(0, ref.shape[0] - 1)]
        pltpu.make_async_copy(all_but_own, all_but_own, sem_a).wait()
        pltpu.make_async_copy(all_but_own, all_but_own, sem_b).wait()


def rotate_kernel(recv_v, rows_v, out, out_v, sems):
    high, low = two_parts(jnp.concatenate([rows_v[:, 0], rows_v[:, 1]], axis=0).T)
    matrix = jnp.concatenate([high, high, low], axis=1)
    width = 256
    stores = []
    for at in range(0, 8 * 128, width):
        columns = []
        for r in range(at // 128, (at + width) // 128):
            values = jnp.concatenate([recv_v[:, 0, r], recv_v[:, 1, r]], axis=0)
            high, low = two_parts(values)
            columns.append(jnp.concatenate([high, low, high], axis=0))
        out_v[:, pl.ds(at, width)] = jnp.dot(
            matrix, jnp.concatenate(columns, axis=1), preferred_element_type=jnp.float32
        )
        store = pltpu.make_async_copy(
            out_v.at[:, pl.ds(at, width)], out.at[:, pl.ds(at, width)], sems.at[at // width]
        )
        store.start()
        stores.append(store)
    for store in stores:
        store.wait()


def per_device(bands, orbitals, potential, subspace):
    orbs, planes = orbitals.shape[0], orbitals.shape[1]
    orb = orbitals.reshape(orbs, planes, 2, 8, 128)
    pot = potential.reshape(planes, 2, 8, 128)
    f32 = jnp.float32
    dma = pltpu.SemaphoreType.DMA
    anywhere = pl.BlockSpec(memory_space=pl.ANY)
    slab, shift = 2 * planes, 2 * REACH
    recv, rows = pl.pallas_call(
        functools.partial(filter_kernel, bands),
        out_shape=(
            pltpu.VMEM((bands * orbs, 8, 128), f32),
            pltpu.VMEM((bands, orbs, 128), f32),
        ),
        in_specs=[anywhere] * 3,
        out_specs=(anywhere,) * 2,
        scratch_shapes=[
            *[
                pltpu.VMEM((slab + 2 * (shift + REACH * (DEG - level)), 2, 8, 128), f32)
                for level in range(DEG)
            ],
            pltpu.VMEM((2 * (slab + 2 * shift), 8, 128), f32),
            pltpu.VMEM((slab + 2 * (shift + REACH * (DEG - 1)), 2, 8, 128), f32),
            dma((2,)),
            dma((2,)),
            dma((2, 5)),
            dma((5,)),
            dma((2,)),
            dma,
            dma((7,)),
            dma((7,)),
            dma((4,)),
            dma,
            dma,
            dma,
            dma,
            pltpu.SemaphoreType.REGULAR,
            pltpu.SemaphoreType.REGULAR,
        ],
        compiler_params=pltpu.CompilerParams(
            collective_id=0, has_side_effects=True, vmem_limit_bytes=32 * 2**20
        ),
        name="filter",
    )(*(pltpu.with_memory_space_constraint(a, pltpu.HBM) for a in (orb, pot, subspace)))
    recv = recv.reshape(bands, orbs, 8, 128)
    return pl.pallas_call(
        rotate_kernel,
        out_shape=jax.ShapeDtypeStruct((bands * orbs, 1024), f32),
        in_specs=[pl.BlockSpec(memory_space=pltpu.VMEM)] * 2,
        out_specs=anywhere,
        scratch_shapes=[pltpu.VMEM((bands * orbs, 1024), f32), dma((4,))],
        compiler_params=pltpu.CompilerParams(vmem_limit_bytes=32 * 2**20),
        name="rotate",
    )(*(pltpu.with_memory_space_constraint(a, pltpu.VMEM) for a in (recv, rows)))


def solution(mesh):
    in_specs = (P("band", "dom", None, None), P("dom", None, None), P("band", None))
    out_specs = P(None, ("dom", "band"))
    return jax.shard_map(
        functools.partial(per_device, mesh.shape["band"]),
        mesh=mesh,
        in_specs=in_specs,
        out_specs=out_specs,
        check_vma=False,
    )
```

profile of v0, /device:TPU:32, one launch (start us, length us, event | category | flops | bytes accessed | tf_op | source)
XLA Modules:
  0.0 38.9 jit_solution(16335199410056401478)
XLA Ops:
  0.0 37.6 %filter.1 = (f32[128,8,128]{2,1,0:T(8,128)S(1)}, f32[64,2,128]{2,1,0:T(2,128)S(1)}) custom-call(f32[2,32,2,8,128]{4,3,2,1,0:T(8,128)} %bitcast.4, f32[32,2,8,128]{3,2,1,0:T(8,128)} %bitcast.5, f32[2,128]{1,0:T(2,128)} %sub.1), custom_call_target="tpu_custom_call" | custom-call | tf_op jit(solution)/shard_map/filter/pallas_call | solution.py:380
  37.6 1.3 %rotate.1 = f32[128,1024]{1,0:T(8,128)} custom-call(f32[64,2,8,128]{3,2,1,0:T(8,128)S(1)} %bitcast.3, f32[64,2,128]{2,1,0:T(2,128)S(1)} %get-tuple-element.8.rows_v), custom_call_target="tpu_custom_call" | custom-call | tf_op jit(solution)/shard_map/rotate/pallas_call | solution.py:417
where the time goes:
time: 39 us; the launch traced here: 38.9 us
  Pallas kernels  38.9 us (100%)
    pallas_call x1, Pallas kernels, per_device(): pl.pallas_call(functools.partial(filter_kernel, bands), out_shape=(pltpu....  37.6 us
    pallas_call x1, Pallas kernels, per_device(): pl.pallas_call(rotate_kernel, out_shape=jax.ShapeDtypeStruct((bands * orb...  1.31 us

commit v1 on v0

--- a/solution.py
+++ b/solution.py
@@ -155,6 +155,32 @@
             device_id=peer, device_id_type=MESH,
         )
 
+    own_rows = pltpu.make_async_copy(sub, rows.at[zl, y, x], move_sem.at[2])
+    own_rows.start()
+    row_lines = [
+        (rows.at[zl, y, x], [{"band": lax.rem(band + d * floor, bands)} for d in range(1, side)]),
+        (rows.at[:, y, x], y_line),
+        (rows.at[:, :, x], [{"band": band - x + lax.rem(x + d, side)} for d in range(1, side)]),
+    ]
+    row_copies = [
+        [
+            remote(
+                sub if stage == 0 else part_rows, part_rows,
+                row_send.at[stage, at], row_recv.at[stage, at], peer,
+            )
+            for at, peer in enumerate(peers)
+        ]
+        for stage, (part_rows, peers) in enumerate(row_lines)
+    ]
+
+    def gather_rows(stage):
+        if stage > 0:
+            for copy in row_copies[stage - 1]:
+                copy.wait_recv()
+        for copy in row_copies[stage]:
+            copy.start()
+
+    gather_rows(0)
     pieces = [(0, REACH)] + [(REACH + 8 * i, 8) for i in range(3)]
     assert sum(n for _, n in pieces) == rims[0]
     far = []
@@ -282,28 +308,6 @@
     apply(2, 20, 3)
     pl.semaphore_wait(all_sem, len(z_line))
 
-    def send_rows(i, c):
-        at = lax.rem(i + band, bands)
-        plane = core * quarter + lax.div(at, 2)
-        plane = jnp.where(
-            left == 1,
-            jnp.where(plane >= slab - shift, plane - slab, plane),
-            jnp.where(plane < shift, plane + slab, plane),
-        )
-        tile = lax.rem(2 * (base + plane) + lax.rem(at, 2) + 2 * whole, 2 * whole)
-
-        @pl.when(tile != own_tile)
-        def _():
-            peer = {"band": lax.rem(tile, bands), "dom": lax.div(tile, bands)}
-            remote(sub, rows.at[band], row_send, row_recv, peer).start()
-
-        return c
-
-    lax.fori_loop(0, bands, send_rows, 0)
-    own_rows = pltpu.make_async_copy(sub, rows.at[band], move_sem.at[2])
-    own_rows.start()
-    spread(20, 24)
-
     pot_far[0].wait_recv()
     passed = [
         remote(mine, mine, pass_send.at[at], pass_recv.at[at], peer)
@@ -319,10 +323,15 @@
     spread(slab - 20, 8)
     for at in range(4):
         if at == 1:
+            own_rows.wait()
+            gather_rows(1)
             for copy in passed:
                 copy.wait_recv()
+        if at == 3:
+            gather_rows(2)
         far[0][at].wait_recv()
         advance(-8 * at)
+    spread(20, 24)
 
     @pl.when(long)
     def _():
@@ -338,12 +347,15 @@
 
     for copy in (near, near_pot, *passed):
         copy.wait_send()
-    own_rows.wait()
+    for copy in row_copies[2]:
+        copy.wait_recv()
+    for copies in row_copies:
+        for copy in copies:
+            copy.wait_send()
     pltpu.make_async_copy(out.at[0], recv.at[row], move_sem.at[3]).wait()
-    for ref, sem_a, sem_b in ((rows, row_send, row_recv), (recv, all_send, all_recv)):
-        all_but_own = ref.at[pl.ds(0, ref.shape[0] - 1)]
-        pltpu.make_async_copy(all_but_own, all_but_own, sem_a).wait()
-        pltpu.make_async_copy(all_but_own, all_but_own, sem_b).wait()
+    all_but_own = recv.at[pl.ds(0, recv.shape[0] - 1)]
+    pltpu.make_async_copy(all_but_own, all_but_own, all_send).wait()
+    pltpu.make_async_copy(all_but_own, all_but_own, all_recv).wait()
 
 
 def rotate_kernel(recv_v, rows_v, out, out_v, sems):
@@ -381,7 +393,7 @@
         functools.partial(filter_kernel, bands),
         out_shape=(
             pltpu.VMEM((bands * orbs, 8, 128), f32),
-            pltpu.VMEM((bands, orbs, 128), f32),
+            pltpu.VMEM((4, 4, 4, orbs, 128), f32),
         ),
         in_specs=[anywhere] * 3,
         out_specs=(anywhere,) * 2,
@@ -403,8 +415,8 @@
             dma((4,)),
             dma,
             dma,
-            dma,
-            dma,
+            dma((3, 3)),
+            dma((3, 3)),
             pltpu.SemaphoreType.REGULAR,
             pltpu.SemaphoreType.REGULAR,
         ],
@@ -413,7 +425,7 @@
         ),
         name="filter",
     )(*(pltpu.with_memory_space_constraint(a, pltpu.HBM) for a in (orb, pot, subspace)))
-    recv = recv.reshape(bands, orbs, 8, 128)
+    recv, rows = recv.reshape(bands, orbs, 8, 128), rows.reshape(bands, orbs, 128)
     return pl.pallas_call(
         rotate_kernel,
         out_shape=jax.ShapeDtypeStruct((bands * orbs, 1024), f32),

time: 39 us -> 40.2 us (1.031)
  the two profiles are of different devices: /device:TPU:32 before, /device:TPU:1 now
where the time goes in v1:
time: 40.2 us; the launch traced here: 40.1 us
  Pallas kernels  40.1 us (100%)
    pallas_call x1, Pallas kernels, per_device(): pl.pallas_call(functools.partial(filter_kernel, bands), out_shape=(pltpu....  38.8 us
    pallas_call x1, Pallas kernels, per_device(): pl.pallas_call(rotate_kernel, out_shape=jax.ShapeDtypeStruct((bands * orb...  1.31 us

profile of v1, /device:TPU:1, one launch (start us, length us, event | category | flops | bytes accessed | tf_op | source)
XLA Modules:
  0.0 40.1 jit_solution(7204907087061987848)
XLA Ops:
  0.0 38.8 %filter.1 = (f32[128,8,128]{2,1,0:T(8,128)S(1)}, f32[4,4,4,2,128]{4,3,2,1,0:T(2,128)S(1)}) custom-call(f32[2,32,2,8,128]{4,3,2,1,0:T(8,128)} %bitcast.6, f32[32,2,8,128]{3,2,1,0:T(8,128)} %bitcast.7, f32[2,128]{1,0:T(2,128)} %sub.1), custom_call_target="tpu_custom_call" | custom-call | tf_op jit(solution)/shard_map/filter/pallas_call | solution.py:392
  38.8 1.3 %rotate.1 = f32[128,1024]{1,0:T(8,128)} custom-call(f32[64,2,8,128]{3,2,1,0:T(8,128)S(1)} %bitcast.4, f32[64,2,128]{2,1,0:T(2,128)S(1)} %bitcast.5), custom_call_target="tpu_custom_call" | custom-call | tf_op jit(solution)/shard_map/rotate/pallas_call | solution.py:429

commit v2 on v1

--- a/solution.py
+++ b/solution.py
@@ -269,7 +269,7 @@
 
     row = 2 * band + core
 
-    def spread(u, count):
+    def spread(u, count, first, number):
         start = placed(u, count)
         tiles = 2 * count
 
@@ -289,12 +289,11 @@
 
             return c
 
-        lax.fori_loop(0, tiles, send, 0)
+        lax.fori_loop(first, first + number, send, 0)
 
     def advance(u):
         for level in range(DEG):
             apply(level, u + level * REACH, 1)
-        spread(u + (DEG - 1) * REACH, 8)
 
     load.wait()
     load_pot.wait()
@@ -307,6 +306,7 @@
     apply(1, 42, 1)
     apply(2, 20, 3)
     pl.semaphore_wait(all_sem, len(z_line))
+    spread(20, 24, 0, 12)
 
     pot_far[0].wait_recv()
     passed = [
@@ -320,7 +320,7 @@
     apply(0, slab - 8, 1)
     apply(1, slab - 14, 1)
     apply(2, slab - 20, 1)
-    spread(slab - 20, 8)
+    spread(slab - 20, 8, 0, 12)
     for at in range(4):
         if at == 1:
             own_rows.wait()
@@ -331,7 +331,19 @@
             gather_rows(2)
         far[0][at].wait_recv()
         advance(-8 * at)
-    spread(20, 24)
+        if at < 3:
+            spread(12 - 8 * at, 8, 0, 12)
+        if at == 1:
+            spread(20, 24, 12, 12)
+
+    def rest(i, c):
+        spread(-12, 8, 4 * i, 4)
+        spread(20, 24, 24 + 6 * i, 6)
+        for u in (slab - 20, 12, 4, -4):
+            spread(u, 8, 12 + i, 1)
+        return c
+
+    lax.fori_loop(0, 4, rest, 0)
 
     @pl.when(long)
     def _():

time: 40.2 us -> 39.5 us (0.983)
  the two profiles are of different devices: /device:TPU:1 before, /device:TPU:32 now
where the time goes in v2:
time: 39.5 us; the launch traced here: 38.8 us
  Pallas kernels  38.8 us (98%)
    pallas_call x1, Pallas kernels, per_device(): pl.pallas_call(functools.partial(filter_kernel, bands), out_shape=(pltpu....  37.5 us
    pallas_call x1, Pallas kernels, per_device(): pl.pallas_call(rotate_kernel, out_shape=jax.ShapeDtypeStruct((bands * orb...  1.31 us

profile of v2, /device:TPU:32, one launch (start us, length us, event | category | flops | bytes accessed | tf_op | source)
XLA Modules:
  0.0 38.8 jit_solution(3209524300164505870)
XLA Ops:
  0.0 37.5 %filter.1 = (f32[128,8,128]{2,1,0:T(8,128)S(1)}, f32[4,4,4,2,128]{4,3,2,1,0:T(2,128)S(1)}) custom-call(f32[2,32,2,8,128]{4,3,2,1,0:T(8,128)} %bitcast.6, f32[32,2,8,128]{3,2,1,0:T(8,128)} %bitcast.7, f32[2,128]{1,0:T(2,128)} %sub.1), custom_call_target="tpu_custom_call" | custom-call | tf_op jit(solution)/shard_map/filter/pallas_call | solution.py:404
  37.5 1.3 %rotate.1 = f32[128,1024]{1,0:T(8,128)} custom-call(f32[64,2,8,128]{3,2,1,0:T(8,128)S(1)} %bitcast.4, f32[64,2,128]{2,1,0:T(2,128)S(1)} %bitcast.5), custom_call_target="tpu_custom_call" | custom-call | tf_op jit(solution)/shard_map/rotate/pallas_call | solution.py:441

commit v3 on v1

--- a/solution.py
+++ b/solution.py
@@ -85,9 +85,9 @@
 
 
 def filter_kernel(
-    bands, orb, pot, sub, recv, rows, p0, p1, p2, out, pot_v,
+    bands, orb, pot, sub, recv, rows, p0, p1, p2, out, given, pot_v,
     near_send, near_recv, far_send, far_recv, pot_send, pot_recv, pass_send, pass_recv,
-    move_sem, all_send, all_recv, row_send, row_recv, plane_sem, all_sem,
+    swap_send, swap_recv, move_sem, all_send, all_recv, row_send, row_recv, plane_sem, all_sem,
 ):
     quarter = orb.shape[1]
     slab, whole = 2 * quarter, 4 * quarter
@@ -262,34 +262,44 @@
             if level < DEG - 1:
                 buffers[level + 1][pl.ds(at + rims[level + 1], step)] = pairs
             else:
-                out[pl.ds(2 * (at + rims[DEG]), 2 * step)] = pairs.reshape(2 * step, 8, 128)
+                keep = jnp.where(core == 0, pairs[:, 0], pairs[:, 1])
+                give = jnp.where(core == 0, pairs[:, 1], pairs[:, 0])
+                out[pl.ds(at + rims[DEG], step), core] = keep
+                given[pl.ds(at + rims[DEG], step)] = give
             return c
 
         lax.fori_loop(0, blocks, body, 0)
 
-    row = 2 * band + core
+    swaps = []
 
     def spread(u, count):
         start = placed(u, count)
-        tiles = 2 * count
+        part = pl.ds(start + rims[DEG], count)
+        number = len(swaps)
+        swap = remote(
+            given.at[part], out.at[part, core], swap_send.at[number], swap_recv.at[number], sibling
+        )
+        swap.start()
+        swaps.append(swap)
+        swap.wait_recv()
 
         def send(i, c):
-            at = lax.rem(i + yx * (tiles // floor), tiles)
-            tile = lax.rem(2 * (base + start) + at + 2 * whole, 2 * whole)
-            src = out.at[2 * (start + rims[DEG]) + at]
+            at = lax.rem(i + yx, count)
+            tile = lax.rem(2 * (base + start + at) + core + 2 * whole, 2 * whole)
+            src = out.at[start + rims[DEG] + at]
 
             @pl.when(tile != own_tile)
             def _():
                 peer = {"band": lax.rem(tile, bands), "dom": lax.div(tile, bands)}
-                remote(src, recv.at[row], all_send, all_recv, peer).start()
+                remote(src, recv.at[band], all_send, all_recv, peer).start()
 
             @pl.when(tile == own_tile)
             def _():
-                pltpu.make_async_copy(src, recv.at[row], move_sem.at[3]).start()
+                pltpu.make_async_copy(src, recv.at[band], move_sem.at[3]).start()
 
             return c
 
-        lax.fori_loop(0, tiles, send, 0)
+        lax.fori_loop(0, count, send, 0)
 
     def advance(u):
         for level in range(DEG):
@@ -307,6 +317,7 @@
     apply(1, 42, 1)
     apply(2, 20, 3)
     pl.semaphore_wait(all_sem, len(z_line))
+    spread(20, 24)
 
     pot_far[0].wait_recv()
     passed = [
@@ -331,7 +342,6 @@
             gather_rows(2)
         far[0][at].wait_recv()
         advance(-8 * at)
-    spread(20, 24)
 
     @pl.when(long)
     def _():
@@ -352,10 +362,22 @@
     for copies in row_copies:
         for copy in copies:
             copy.wait_send()
-    pltpu.make_async_copy(out.at[0], recv.at[row], move_sem.at[3]).wait()
-    all_but_own = recv.at[pl.ds(0, recv.shape[0] - 1)]
-    pltpu.make_async_copy(all_but_own, all_but_own, all_send).wait()
-    pltpu.make_async_copy(all_but_own, all_but_own, all_recv).wait()
+    for swap in swaps:
+        swap.wait_send()
+
+    def finish(number):
+        arrived = recv.at[pl.ds(0, number)]
+        pltpu.make_async_copy(arrived, arrived, all_send).wait()
+        pltpu.make_async_copy(arrived, arrived, all_recv).wait()
+
+    @pl.when(lax.rem(x, 2) == core)
+    def _():
+        pltpu.make_async_copy(out.at[0], recv.at[0], move_sem.at[3]).wait()
+        finish(bands - 1)
+
+    @pl.when(lax.rem(x, 2) != core)
+    def _():
+        finish(bands)
 
 
 def rotate_kernel(recv_v, rows_v, out, out_v, sems):
@@ -392,7 +414,7 @@
     recv, rows = pl.pallas_call(
         functools.partial(filter_kernel, bands),
         out_shape=(
-            pltpu.VMEM((bands * orbs, 8, 128), f32),
+            pltpu.VMEM((bands, orbs, 8, 128), f32),
             pltpu.VMEM((4, 4, 4, orbs, 128), f32),
         ),
         in_specs=[anywhere] * 3,
@@ -402,7 +424,8 @@
                 pltpu.VMEM((slab + 2 * (shift + REACH * (DEG - level)), 2, 8, 128), f32)
                 for level in range(DEG)
             ],
-            pltpu.VMEM((2 * (slab + 2 * shift), 8, 128), f32),
+            pltpu.VMEM((slab + 2 * shift, orbs, 8, 128), f32),
+            pltpu.VMEM((slab + 2 * shift, 8, 128), f32),
             pltpu.VMEM((slab + 2 * (shift + REACH * (DEG - 1)), 2, 8, 128), f32),
             dma((2,)),
             dma((2,)),
@@ -412,6 +435,8 @@
             dma,
             dma((7,)),
             dma((7,)),
+            dma((6,)),
+            dma((6,)),
             dma((4,)),
             dma,
             dma,
@@ -425,7 +450,7 @@
         ),
         name="filter",
     )(*(pltpu.with_memory_space_constraint(a, pltpu.HBM) for a in (orb, pot, subspace)))
-    recv, rows = recv.reshape(bands, orbs, 8, 128), rows.reshape(bands, orbs, 128)
+    rows = rows.reshape(bands, orbs, 128)
     return pl.pallas_call(
         rotate_kernel,
         out_shape=jax.ShapeDtypeStruct((bands * orbs, 1024), f32),

time: 40.2 us -> 40.1 us (level)
  the two profiles are of different devices: /device:TPU:1 before, /device:TPU:32 now
where the time goes in v3:
time: 40.1 us; the launch traced here: 40 us
  Pallas kernels  40 us (100%)
    pallas_call x1, Pallas kernels, per_device(): pl.pallas_call(functools.partial(filter_kernel, bands), out_shape=(pltpu....  38.7 us
    pallas_call x1, Pallas kernels, per_device(): pl.pallas_call(rotate_kernel, out_shape=jax.ShapeDtypeStruct((bands * orb...  1.31 us

profile of v3, /device:TPU:32, one launch (start us, length us, event | category | flops | bytes accessed | tf_op | source)
XLA Modules:
  0.0 40.0 jit_solution(12999257883439561993)
XLA Ops:
  0.0 38.7 %filter.1 = (f32[64,2,8,128]{3,2,1,0:T(8,128)S(1)}, f32[4,4,4,2,128]{4,3,2,1,0:T(2,128)S(1)}) custom-call(f32[2,32,2,8,128]{4,3,2,1,0:T(8,128)} %bitcast.4, f32[32,2,8,128]{3,2,1,0:T(8,128)} %bitcast.5, f32[2,128]{1,0:T(2,128)} %sub.1), custom_call_target="tpu_custom_call" | custom-call | tf_op jit(solution)/shard_map/filter/pallas_call | solution.py:414
  38.7 1.3 %rotate.1 = f32[128,1024]{1,0:T(8,128)} custom-call(f32[64,2,8,128]{3,2,1,0:T(8,128)S(1)} %get-tuple-element.7.recv_v, f32[64,2,128]{2,1,0:T(2,128)S(1)} %bitcast.3), custom_call_target="tpu_custom_call" | custom-call | tf_op jit(solution)/shard_map/rotate/pallas_call | solution.py:454

commit v4 on v3

--- a/solution.py
+++ b/solution.py
@@ -218,8 +218,9 @@
     def _():
         for o in range(2):
             pot_far[o].start()
-        for o in range(2):
-            far[o][0].start()
+        for at in range(4):
+            for o in range(2):
+                far[o][at].start()
 
     @pl.when(jnp.logical_not(long))
     def _():
@@ -236,12 +237,6 @@
     )
     near.start()
     near_pot.start()
-
-    @pl.when(long)
-    def _():
-        for at in range(1, 4):
-            for o in range(2):
-                far[o][at].start()
 
     tell(y_line, plane_sem)
 

time: 40.1 us -> 40.1 us (level)
  no operation moved by 1% of the time
where the time goes in v4:
time: 40.1 us; the launch traced here: 40 us
  Pallas kernels  40 us (100%)
    pallas_call x1, Pallas kernels, per_device(): pl.pallas_call(functools.partial(filter_kernel, bands), out_shape=(pltpu....  38.7 us
    pallas_call x1, Pallas kernels, per_device(): pl.pallas_call(rotate_kernel, out_shape=jax.ShapeDtypeStruct((bands * orb...  1.31 us

profile of v4, /device:TPU:32, one launch (start us, length us, event | category | flops | bytes accessed | tf_op | source)
XLA Modules:
  0.0 40.0 jit_solution(16351662788010264706)
XLA Ops:
  0.0 38.7 %filter.1 = (f32[64,2,8,128]{3,2,1,0:T(8,128)S(1)}, f32[4,4,4,2,128]{4,3,2,1,0:T(2,128)S(1)}) custom-call(f32[2,32,2,8,128]{4,3,2,1,0:T(8,128)} %bitcast.4, f32[32,2,8,128]{3,2,1,0:T(8,128)} %bitcast.5, f32[2,128]{1,0:T(2,128)} %sub.1), custom_call_target="tpu_custom_call" | custom-call | tf_op jit(solution)/shard_map/filter/pallas_call | solution.py:409
  38.7 1.3 %rotate.1 = f32[128,1024]{1,0:T(8,128)} custom-call(f32[64,2,8,128]{3,2,1,0:T(8,128)S(1)} %get-tuple-element.7.recv_v, f32[64,2,128]{2,1,0:T(2,128)S(1)} %bitcast.3), custom_call_target="tpu_custom_call" | custom-call | tf_op jit(solution)/shard_map/rotate/pallas_call | solution.py:449

commit v5 on v4

--- a/solution.py
+++ b/solution.py
@@ -183,26 +183,28 @@
     gather_rows(0)
     pieces = [(0, REACH)] + [(REACH + 8 * i, 8) for i in range(3)]
     assert sum(n for _, n in pieces) == rims[0]
-    far = []
+    far, far_parts = [], []
     for o in range(2):
-        group = []
-        for at, (a, n) in enumerate(pieces):
-            group.append(
+        group, group_parts = [], []
+        for at, (a, n) in enumerate(pieces + [(slab, REACH)]):
+            if a < slab:
+                source = jnp.where(left == 1, quarter - a - n, a)
+                target = placed(-a - n, n) + rims[0]
+            else:
+                source = jnp.where(left == 1, 0, quarter - n)
+                target = placed(a, n) + rims[0]
+            copies = [
                 remote(
-                    orb.at[o, pl.ds(jnp.where(left == 1, quarter - a - n, a), n)],
-                    p0.at[pl.ds(placed(-a - n, n) + rims[0], n)],
+                    orb.at[o, pl.ds(source + i, size)], p0.at[pl.ds(target + i, size)],
                     far_send.at[o, at], far_recv.at[at], partners[o],
                 )
-            )
-        n = REACH
-        group.append(
-            remote(
-                orb.at[o, pl.ds(jnp.where(left == 1, 0, quarter - n), n)],
-                p0.at[pl.ds(placed(slab, n) + rims[0], n)],
-                far_send.at[o, 4], far_recv.at[4], partners[o],
-            )
-        )
+                for size, places in ((n, (0,)), (2, range(0, n, 2)))
+                for i in places
+            ]
+            group.append(copies[0])
+            group_parts.append(copies[1:])
         far.append(group)
+        far_parts.append(group_parts)
     part = pot_rim // 8
     pot_far = [
         remote(
@@ -220,23 +222,34 @@
             pot_far[o].start()
         for at in range(4):
             for o in range(2):
-                far[o][at].start()
+                for copy in far_parts[o][at]:
+                    copy.start()
 
     @pl.when(jnp.logical_not(long))
     def _():
         for o in range(2):
-            far[o][4].start()
-
-    near = remote(
-        orb.at[1 - core], p0.at[pl.ds(core * quarter + rims[0], quarter)],
-        near_send.at[0], near_recv.at[0], sibling,
-    )
-    near_pot = remote(
-        pot, pot_v.at[pl.ds(core * quarter + pot_rim, quarter)],
-        near_send.at[1], near_recv.at[1], sibling,
-    )
-    near.start()
-    near_pot.start()
+            for copy in far_parts[o][4]:
+                copy.start()
+
+    near, *near_parts = [
+        remote(
+            orb.at[1 - core, pl.ds(i, size)],
+            p0.at[pl.ds(core * quarter + rims[0] + i, size)],
+            near_send.at[0], near_recv.at[0], sibling,
+        )
+        for size, places in ((quarter, (0,)), (4, range(0, quarter, 4)))
+        for i in places
+    ]
+    near_pot, *near_pot_parts = [
+        remote(
+            pot.at[pl.ds(i, size)], pot_v.at[pl.ds(core * quarter + pot_rim + i, size)],
+            near_send.at[1], near_recv.at[1], sibling,
+        )
+        for size, places in ((quarter, (0,)), (4, range(0, quarter, 4)))
+        for i in places
+    ]
+    for copy in (*near_parts, *near_pot_parts):
+        copy.start()
 
     tell(y_line, plane_sem)
 

time: 40.1 us -> 40.1 us (level)
  no operation moved by 1% of the time
where the time goes in v5:
time: 40.1 us; the launch traced here: 40 us
  Pallas kernels  40 us (100%)
    pallas_call x1, Pallas kernels, per_device(): pl.pallas_call(functools.partial(filter_kernel, bands), out_shape=(pltpu....  38.7 us
    pallas_call x1, Pallas kernels, per_device(): pl.pallas_call(rotate_kernel, out_shape=jax.ShapeDtypeStruct((bands * orb...  1.31 us

profile of v5, /device:TPU:32, one launch (start us, length us, event | category | flops | bytes accessed | tf_op | source)
XLA Modules:
  0.0 40.0 jit_solution(9622972188469778975)
XLA Ops:
  0.0 38.7 %filter.1 = (f32[64,2,8,128]{3,2,1,0:T(8,128)S(1)}, f32[4,4,4,2,128]{4,3,2,1,0:T(2,128)S(1)}) custom-call(f32[2,32,2,8,128]{4,3,2,1,0:T(8,128)} %bitcast.4, f32[32,2,8,128]{3,2,1,0:T(8,128)} %bitcast.5, f32[2,128]{1,0:T(2,128)} %sub.1), custom_call_target="tpu_custom_call" | custom-call | tf_op jit(solution)/shard_map/filter/pallas_call | solution.py:422
  38.7 1.3 %rotate.1 = f32[128,1024]{1,0:T(8,128)} custom-call(f32[64,2,8,128]{3,2,1,0:T(8,128)S(1)} %get-tuple-element.7.recv_v, f32[64,2,128]{2,1,0:T(2,128)S(1)} %bitcast.3), custom_call_target="tpu_custom_call" | custom-call | tf_op jit(solution)/shard_map/rotate/pallas_call | solution.py:462

commit v6 on v1

--- a/solution.py
+++ b/solution.py
@@ -48,15 +48,15 @@
     return high, (values - high.astype(jnp.float32)).astype(jnp.bfloat16)
 
 
-def stencil_matrix(period, axis):
-    rows = lax.broadcasted_iota(jnp.int32, (128, 128), 0)
-    columns = lax.broadcasted_iota(jnp.int32, (128, 128), 1)
+def stencil_matrix(size, period, axis):
+    rows = lax.broadcasted_iota(jnp.int32, (size, size), 0)
+    columns = lax.broadcasted_iota(jnp.int32, (size, size), 1)
     apart = jnp.abs(rows - columns)
-    if period < 128:
+    if period < size:
         same = jnp.bitwise_or(rows, period - 1) == jnp.bitwise_or(columns, period - 1)
         apart = jnp.where(same, apart, 0)
     apart = jnp.minimum(apart, period - apart)
-    matrix = jnp.zeros((128, 128), jnp.float32)
+    matrix = jnp.zeros((size, size), jnp.float32)
     for k, w in enumerate(stencil_weights()[1], 1):
         matrix = jnp.where(apart == k, jnp.float32(w), matrix)
     high, low = two_parts(matrix)
@@ -146,7 +146,8 @@
             pl.semaphore_signal(semaphore, inc=1, device_id=peer, device_id_type=MESH)
 
     tell(entered, barrier)
-    lanes, lines = stencil_matrix(128, 0), stencil_matrix(16, 1)
+    lanes = stencil_matrix(128, 128, 0)
+    lines = {n: stencil_matrix(16 * n, 16, 1) for n in (4, 8)}
     pl.semaphore_wait(barrier, len(entered))
 
     def remote(src, dst, send_sem, recv_sem, peer):
@@ -181,7 +182,7 @@
             copy.start()
 
     gather_rows(0)
-    pieces = [(0, REACH)] + [(REACH + 8 * i, 8) for i in range(3)]
+    pieces = [(0, 6), (6, 8), (14, 8), (22, 4), (26, 4)]
     assert sum(n for _, n in pieces) == rims[0]
     far = []
     for o in range(2):
@@ -199,7 +200,7 @@
             remote(
                 orb.at[o, pl.ds(jnp.where(left == 1, 0, quarter - n), n)],
                 p0.at[pl.ds(placed(slab, n) + rims[0], n)],
-                far_send.at[o, 4], far_recv.at[4], partners[o],
+                far_send.at[o, 5], far_recv.at[5], partners[o],
             )
         )
         far.append(group)
@@ -218,13 +219,14 @@
     def _():
         for o in range(2):
             pot_far[o].start()
-        for o in range(2):
-            far[o][0].start()
+        for at in range(len(pieces)):
+            for o in range(2):
+                far[o][at].start()
 
     @pl.when(jnp.logical_not(long))
     def _():
         for o in range(2):
-            far[o][4].start()
+            far[o][5].start()
 
     near = remote(
         orb.at[1 - core], p0.at[pl.ds(core * quarter + rims[0], quarter)],
@@ -237,17 +239,9 @@
     near.start()
     near_pot.start()
 
-    @pl.when(long)
-    def _():
-        for at in range(1, 4):
-            for o in range(2):
-                far[o][at].start()
-
     tell(y_line, plane_sem)
 
-    step = 8
-
-    def apply(level, u, blocks):
+    def apply(level, u, blocks, step=8):
         scale, weight = scalars[level]
 
         def body(i, c):
@@ -257,7 +251,7 @@
                 before = buffers[level - 1][pl.ds(at + rims[level - 1], step)]
             window = buffers[level][pl.ds(at + rims[level] - REACH, step + 2 * REACH)]
             pairs = filtered_block(
-                window, pot_v[pl.ds(at + pot_rim, step)], before, scale, weight, lanes, lines
+                window, pot_v[pl.ds(at + pot_rim, step)], before, scale, weight, lanes, lines[step]
             )
             if level < DEG - 1:
                 buffers[level + 1][pl.ds(at + rims[level + 1], step)] = pairs
@@ -274,7 +268,7 @@
         tiles = 2 * count
 
         def send(i, c):
-            at = lax.rem(i + yx * (tiles // floor), tiles)
+            at = lax.rem(i + yx * max(tiles // floor, 1), tiles)
             tile = lax.rem(2 * (base + start) + at + 2 * whole, 2 * whole)
             src = out.at[2 * (start + rims[DEG]) + at]
 
@@ -291,10 +285,10 @@
 
         lax.fori_loop(0, tiles, send, 0)
 
-    def advance(u):
+    def advance(u, n):
         for level in range(DEG):
-            apply(level, u + level * REACH, 1)
-        spread(u + (DEG - 1) * REACH, 8)
+            apply(level, u + level * REACH, 1, n)
+        spread(u + (DEG - 1) * REACH, n)
 
     load.wait()
     load_pot.wait()
@@ -307,6 +301,7 @@
     apply(1, 42, 1)
     apply(2, 20, 3)
     pl.semaphore_wait(all_sem, len(z_line))
+    spread(20, 24)
 
     pot_far[0].wait_recv()
     passed = [
@@ -316,12 +311,12 @@
     for copy in passed:
         copy.start()
 
-    far[0][4].wait_recv()
+    far[0][5].wait_recv()
     apply(0, slab - 8, 1)
     apply(1, slab - 14, 1)
     apply(2, slab - 20, 1)
     spread(slab - 20, 8)
-    for at in range(4):
+    for at, (u, n) in enumerate(((0, 8), (-8, 8), (-16, 8), (-20, 4), (-24, 4))):
         if at == 1:
             own_rows.wait()
             gather_rows(1)
@@ -330,20 +325,19 @@
         if at == 3:
             gather_rows(2)
         far[0][at].wait_recv()
-        advance(-8 * at)
-    spread(20, 24)
+        advance(u, n)
 
     @pl.when(long)
     def _():
         for o in range(2):
             pot_far[o].wait_send()
-            for at in range(4):
+            for at in range(len(pieces)):
                 far[o][at].wait_send()
 
     @pl.when(jnp.logical_not(long))
     def _():
         for o in range(2):
-            far[o][4].wait_send()
+            far[o][5].wait_send()
 
     for copy in (near, near_pot, *passed):
         copy.wait_send()
@@ -406,8 +400,8 @@
             pltpu.VMEM((slab + 2 * (shift + REACH * (DEG - 1)), 2, 8, 128), f32),
             dma((2,)),
             dma((2,)),
-            dma((2, 5)),
-            dma((5,)),
+            dma((2, 6)),
+            dma((6,)),
             dma((2,)),
             dma,
             dma((7,)),

time: 40.2 us -> 38.6 us (0.960)
  the two profiles are of different devices: /device:TPU:1 before, /device:TPU:32 now
where the time goes in v6:
time: 38.6 us; the launch traced here: 38.5 us
  Pallas kernels  38.5 us (100%)
    pallas_call x1, Pallas kernels, per_device(): pl.pallas_call(functools.partial(filter_kernel, bands), out_shape=(pltpu....  37.2 us
    pallas_call x1, Pallas kernels, per_device(): pl.pallas_call(rotate_kernel, out_shape=jax.ShapeDtypeStruct((bands * orb...  1.31 us

profile of v6, /device:TPU:32, one launch (start us, length us, event | category | flops | bytes accessed | tf_op | source)
XLA Modules:
  0.0 38.5 jit_solution(7675060363072518980)
XLA Ops:
  0.0 37.2 %filter.1 = (f32[128,8,128]{2,1,0:T(8,128)S(1)}, f32[4,4,4,2,128]{4,3,2,1,0:T(2,128)S(1)}) custom-call(f32[2,32,2,8,128]{4,3,2,1,0:T(8,128)} %bitcast.6, f32[32,2,8,128]{3,2,1,0:T(8,128)} %bitcast.7, f32[2,128]{1,0:T(2,128)} %sub.1), custom_call_target="tpu_custom_call" | custom-call | tf_op jit(solution)/shard_map/filter/pallas_call | solution.py:386
  37.2 1.3 %rotate.1 = f32[128,1024]{1,0:T(8,128)} custom-call(f32[64,2,8,128]{3,2,1,0:T(8,128)S(1)} %bitcast.4, f32[64,2,128]{2,1,0:T(2,128)S(1)} %bitcast.5), custom_call_target="tpu_custom_call" | custom-call | tf_op jit(solution)/shard_map/rotate/pallas_call | solution.py:423

commit v7 on v6

--- a/solution.py
+++ b/solution.py
@@ -290,8 +290,18 @@
             apply(level, u + level * REACH, 1, n)
         spread(u + (DEG - 1) * REACH, n)
 
+    pot_far[0].wait_recv()
+    passed = [
+        remote(mine, mine, pass_send.at[at], pass_recv.at[at], peer)
+        for at, peer in enumerate(x_line)
+    ]
+    for copy in passed:
+        copy.start()
+
     load.wait()
     load_pot.wait()
+    own_rows.wait()
+    gather_rows(1)
     near.wait_recv()
     near_pot.wait_recv()
     pl.semaphore_wait(plane_sem, len(y_line))
@@ -300,16 +310,9 @@
     apply(1, 14, 4)
     apply(1, 42, 1)
     apply(2, 20, 3)
+    gather_rows(2)
     pl.semaphore_wait(all_sem, len(z_line))
     spread(20, 24)
-
-    pot_far[0].wait_recv()
-    passed = [
-        remote(mine, mine, pass_send.at[at], pass_recv.at[at], peer)
-        for at, peer in enumerate(x_line)
-    ]
-    for copy in passed:
-        copy.start()
 
     far[0][5].wait_recv()
     apply(0, slab - 8, 1)
@@ -318,12 +321,8 @@
     spread(slab - 20, 8)
     for at, (u, n) in enumerate(((0, 8), (-8, 8), (-16, 8), (-20, 4), (-24, 4))):
         if at == 1:
-            own_rows.wait()
-            gather_rows(1)
             for copy in passed:
                 copy.wait_recv()
-        if at == 3:
-            gather_rows(2)
         far[0][at].wait_recv()
         advance(u, n)
 

time: 38.6 us -> 37.2 us (0.964)
  Pallas kernels: 38.5 us -> 37.2 us
    pallas_call x1, Pallas kernels: 37.2 us -> 35.9 us  [per_device(): pl.pallas_call(functools.partial(filter_kernel, bands), out_shape=(pltpu....]
where the time goes in v7:
time: 37.2 us
  Pallas kernels  37.2 us (100%)
    pallas_call x1, Pallas kernels, per_device(): pl.pallas_call(functools.partial(filter_kernel, bands), out_shape=(pltpu....  35.9 us
    pallas_call x1, Pallas kernels, per_device(): pl.pallas_call(rotate_kernel, out_shape=jax.ShapeDtypeStruct((bands * orb...  1.31 us

profile of v7, /device:TPU:32, one launch (start us, length us, event | category | flops | bytes accessed | tf_op | source)
XLA Modules:
  0.0 37.2 jit_solution(4061388242183896267)
XLA Ops:
  0.0 35.9 %filter.1 = (f32[128,8,128]{2,1,0:T(8,128)S(1)}, f32[4,4,4,2,128]{4,3,2,1,0:T(2,128)S(1)}) custom-call(f32[2,32,2,8,128]{4,3,2,1,0:T(8,128)} %bitcast.6, f32[32,2,8,128]{3,2,1,0:T(8,128)} %bitcast.7, f32[2,128]{1,0:T(2,128)} %sub.1), custom_call_target="tpu_custom_call" | custom-call | tf_op jit(solution)/shard_map/filter/pallas_call | solution.py:385
  35.9 1.3 %rotate.1 = f32[128,1024]{1,0:T(8,128)} custom-call(f32[64,2,8,128]{3,2,1,0:T(8,128)S(1)} %bitcast.4, f32[64,2,128]{2,1,0:T(2,128)S(1)} %bitcast.5), custom_call_target="tpu_custom_call" | custom-call | tf_op jit(solution)/shard_map/rotate/pallas_call | solution.py:422

commit v8 on v7

--- a/solution.py
+++ b/solution.py
@@ -259,31 +259,36 @@
                 out[pl.ds(2 * (at + rims[DEG]), 2 * step)] = pairs.reshape(2 * step, 8, 128)
             return c
 
-        lax.fori_loop(0, blocks, body, 0)
+        lax.fori_loop(0, blocks, body, 0, unroll=min(blocks, 3))
 
     row = 2 * band + core
+    offsets = [lax.rem(i + yx, 8) for i in range(8)]
 
     def spread(u, count):
         start = placed(u, count)
-        tiles = 2 * count
-
-        def send(i, c):
-            at = lax.rem(i + yx * max(tiles // floor, 1), tiles)
-            tile = lax.rem(2 * (base + start) + at + 2 * whole, 2 * whole)
-            src = out.at[2 * (start + rims[DEG]) + at]
-
-            @pl.when(tile != own_tile)
-            def _():
-                peer = {"band": lax.rem(tile, bands), "dom": lax.div(tile, bands)}
-                remote(src, recv.at[row], all_send, all_recv, peer).start()
-
-            @pl.when(tile == own_tile)
-            def _():
-                pltpu.make_async_copy(src, recv.at[row], move_sem.at[3]).start()
+        groups = count // 4
+
+        def send_group(i, c):
+            plane = start + 4 * lax.rem(i + yx, groups)
+            tile = lax.rem(2 * (base + plane) + 2 * whole, 2 * whole)
+            there, first = lax.div(tile, bands), lax.rem(tile, bands)
+            place = 2 * (plane + rims[DEG])
+            for offset in offsets:
+                src, peer = out.at[place + offset], first + offset
+
+                @pl.when((peer != band) | (there != dom))
+                def _():
+                    remote(
+                        src, recv.at[row], all_send, all_recv, {"band": peer, "dom": there}
+                    ).start()
+
+                @pl.when((peer == band) & (there == dom))
+                def _():
+                    pltpu.make_async_copy(src, recv.at[row], move_sem.at[3]).start()
 
             return c
 
-        lax.fori_loop(0, tiles, send, 0)
+        lax.fori_loop(0, groups, send_group, 0)
 
     def advance(u, n):
         for level in range(DEG):

time: 37.2 us -> 38.1 us (1.024)
  Pallas kernels: 37.2 us -> 38 us
    pallas_call x1, Pallas kernels: 35.9 us -> 36.7 us  [per_device(): pl.pallas_call(functools.partial(filter_kernel, bands), out_shape=(pltpu....]
where the time goes in v8:
time: 38.1 us; the launch traced here: 38 us
  Pallas kernels  38 us (100%)
    pallas_call x1, Pallas kernels, per_device(): pl.pallas_call(functools.partial(filter_kernel, bands), out_shape=(pltpu....  36.7 us
    pallas_call x1, Pallas kernels, per_device(): pl.pallas_call(rotate_kernel, out_shape=jax.ShapeDtypeStruct((bands * orb...  1.31 us

profile of v8, /device:TPU:32, one launch (start us, length us, event | category | flops | bytes accessed | tf_op | source)
XLA Modules:
  0.0 38.0 jit_solution(7255149879163909412)
XLA Ops:
  0.0 36.7 %filter.1 = (f32[128,8,128]{2,1,0:T(8,128)S(1)}, f32[4,4,4,2,128]{4,3,2,1,0:T(2,128)S(1)}) custom-call(f32[2,32,2,8,128]{4,3,2,1,0:T(8,128)} %bitcast.6, f32[32,2,8,128]{3,2,1,0:T(8,128)} %bitcast.7, f32[2,128]{1,0:T(2,128)} %sub.1), custom_call_target="tpu_custom_call" | custom-call | tf_op jit(solution)/shard_map/filter/pallas_call | solution.py:390
  36.7 1.3 %rotate.1 = f32[128,1024]{1,0:T(8,128)} custom-call(f32[64,2,8,128]{3,2,1,0:T(8,128)S(1)} %bitcast.4, f32[64,2,128]{2,1,0:T(2,128)S(1)} %bitcast.5), custom_call_target="tpu_custom_call" | custom-call | tf_op jit(solution)/shard_map/rotate/pallas_call | solution.py:427

commit v9 on v7

--- a/solution.py
+++ b/solution.py
@@ -147,7 +147,7 @@
 
     tell(entered, barrier)
     lanes = stencil_matrix(128, 128, 0)
-    lines = {n: stencil_matrix(16 * n, 16, 1) for n in (4, 8)}
+    lines = stencil_matrix(128, 16, 1)
     pl.semaphore_wait(barrier, len(entered))
 
     def remote(src, dst, send_sem, recv_sem, peer):
@@ -182,7 +182,7 @@
             copy.start()
 
     gather_rows(0)
-    pieces = [(0, 6), (6, 8), (14, 8), (22, 4), (26, 4)]
+    pieces = [(0, 6), (6, 8), (14, 8), (22, 8)]
     assert sum(n for _, n in pieces) == rims[0]
     far = []
     for o in range(2):
@@ -200,7 +200,7 @@
             remote(
                 orb.at[o, pl.ds(jnp.where(left == 1, 0, quarter - n), n)],
                 p0.at[pl.ds(placed(slab, n) + rims[0], n)],
-                far_send.at[o, 5], far_recv.at[5], partners[o],
+                far_send.at[o, 4], far_recv.at[4], partners[o],
             )
         )
         far.append(group)
@@ -226,7 +226,7 @@
     @pl.when(jnp.logical_not(long))
     def _():
         for o in range(2):
-            far[o][5].start()
+            far[o][4].start()
 
     near = remote(
         orb.at[1 - core], p0.at[pl.ds(core * quarter + rims[0], quarter)],
@@ -241,25 +241,26 @@
 
     tell(y_line, plane_sem)
 
-    def apply(level, u, blocks, step=8):
+    step = 8
+
+    def apply(level, *places):
         scale, weight = scalars[level]
-
-        def body(i, c):
-            at = placed(u + i * step, step)
+        begins = [placed(u, step) for u in places]
+        results = []
+        for at in begins:
             before = None
             if level > 0:
                 before = buffers[level - 1][pl.ds(at + rims[level - 1], step)]
             window = buffers[level][pl.ds(at + rims[level] - REACH, step + 2 * REACH)]
             pairs = filtered_block(
-                window, pot_v[pl.ds(at + pot_rim, step)], before, scale, weight, lanes, lines[step]
+                window, pot_v[pl.ds(at + pot_rim, step)], before, scale, weight, lanes, lines
             )
+            results.append(pairs)
+        for at, pairs in zip(begins, results):
             if level < DEG - 1:
                 buffers[level + 1][pl.ds(at + rims[level + 1], step)] = pairs
             else:
                 out[pl.ds(2 * (at + rims[DEG]), 2 * step)] = pairs.reshape(2 * step, 8, 128)
-            return c
-
-        lax.fori_loop(0, blocks, body, 0)
 
     row = 2 * band + core
 
@@ -284,11 +285,6 @@
             return c
 
         lax.fori_loop(0, tiles, send, 0)
-
-    def advance(u, n):
-        for level in range(DEG):
-            apply(level, u + level * REACH, 1, n)
-        spread(u + (DEG - 1) * REACH, n)
 
     pot_far[0].wait_recv()
     passed = [
@@ -306,25 +302,31 @@
     near_pot.wait_recv()
     pl.semaphore_wait(plane_sem, len(y_line))
     tell(z_line, all_sem)
-    apply(0, 8, 6)
-    apply(1, 14, 4)
-    apply(1, 42, 1)
-    apply(2, 20, 3)
+    apply(0, 8, 16, 24)
+    apply(0, 32, 40, 48)
+    apply(1, 14, 22)
+    apply(1, 30, 38, 42)
+    apply(2, 20, 28, 36)
     gather_rows(2)
     pl.semaphore_wait(all_sem, len(z_line))
     spread(20, 24)
 
-    far[0][5].wait_recv()
-    apply(0, slab - 8, 1)
-    apply(1, slab - 14, 1)
-    apply(2, slab - 20, 1)
-    spread(slab - 20, 8)
-    for at, (u, n) in enumerate(((0, 8), (-8, 8), (-16, 8), (-20, 4), (-24, 4))):
-        if at == 1:
-            for copy in passed:
-                copy.wait_recv()
+    for at in (4, 0, 1):
         far[0][at].wait_recv()
-        advance(u, n)
+    for copy in passed:
+        copy.wait_recv()
+    apply(0, -8, 0, slab - 8)
+    apply(1, -2, 6, slab - 14)
+    apply(2, 4, 12, slab - 20)
+    for u in (4, 12, slab - 20):
+        spread(u, 8)
+    for at in (2, 3):
+        far[0][at].wait_recv()
+    apply(0, -24, -16)
+    apply(1, -18, -10)
+    apply(2, -12, -4)
+    spread(-12, 8)
+    spread(-4, 8)
 
     @pl.when(long)
     def _():
@@ -336,7 +338,7 @@
     @pl.when(jnp.logical_not(long))
     def _():
         for o in range(2):
-            far[o][5].wait_send()
+            far[o][4].wait_send()
 
     for copy in (near, near_pot, *passed):
         copy.wait_send()
@@ -399,8 +401,8 @@
             pltpu.VMEM((slab + 2 * (shift + REACH * (DEG - 1)), 2, 8, 128), f32),
             dma((2,)),
             dma((2,)),
-            dma((2, 6)),
-            dma((6,)),
+            dma((2, 5)),
+            dma((5,)),
             dma((2,)),
             dma,
             dma((7,)),

time: 37.2 us -> 39.2 us (1.054)
  the two profiles are of different devices: /device:TPU:32 before, /device:TPU:8 now
where the time goes in v9:
time: 39.2 us; the launch traced here: 39.1 us
  Pallas kernels  39.1 us (100%)
    pallas_call x1, Pallas kernels, per_device(): pl.pallas_call(functools.partial(filter_kernel, bands), out_shape=(pltpu....  37.8 us
    pallas_call x1, Pallas kernels, per_device(): pl.pallas_call(rotate_kernel, out_shape=jax.ShapeDtypeStruct((bands * orb...  1.31 us

profile of v9, /device:TPU:8, one launch (start us, length us, event | category | flops | bytes accessed | tf_op | source)
XLA Modules:
  0.0 39.1 jit_solution(984280273503950367)
XLA Ops:
  0.0 37.8 %filter.1 = (f32[128,8,128]{2,1,0:T(8,128)S(1)}, f32[4,4,4,2,128]{4,3,2,1,0:T(2,128)S(1)}) custom-call(f32[2,32,2,8,128]{4,3,2,1,0:T(8,128)} %bitcast.6, f32[32,2,8,128]{3,2,1,0:T(8,128)} %bitcast.7, f32[2,128]{1,0:T(2,128)} %sub.1), custom_call_target="tpu_custom_call" | custom-call | tf_op jit(solution)/shard_map/filter/pallas_call | solution.py:387
  37.8 1.3 %rotate.1 = f32[128,1024]{1,0:T(8,128)} custom-call(f32[64,2,8,128]{3,2,1,0:T(8,128)S(1)} %bitcast.4, f32[64,2,128]{2,1,0:T(2,128)S(1)} %bitcast.5), custom_call_target="tpu_custom_call" | custom-call | tf_op jit(solution)/shard_map/rotate/pallas_call | solution.py:424

commit v10 on v7

--- a/solution.py
+++ b/solution.py
@@ -85,8 +85,8 @@
 
 
 def filter_kernel(
-    bands, orb, pot, sub, recv, rows, p0, p1, p2, out, pot_v,
-    near_send, near_recv, far_send, far_recv, pot_send, pot_recv, pass_send, pass_recv,
+    bands, orb, pot, sub, recv, matrix, rows, p0, p1, p2, out, pot_v,
+    near_send, near_recv, far_send, far_recv, pot_send, pot_recv, pair_send, pair_recv, pass_send, pass_recv,
     move_sem, all_send, all_recv, row_send, row_recv, plane_sem, all_sem,
 ):
     quarter = orb.shape[1]
@@ -205,10 +205,15 @@
         )
         far.append(group)
     part = pot_rim // 8
+    parity = lax.rem(y, 2)
     pot_far = [
         remote(
-            pot.at[pl.ds(jnp.where(left == 1, quarter - pot_rim, 0) + (2 * x + o) * part, part)],
-            pot_v.at[pl.ds(placed(-pot_rim, pot_rim) + pot_rim + (2 * x + o) * part, part)],
+            pot.at[
+                pl.ds(jnp.where(left == 1, quarter - pot_rim, 0) + (2 * x + o) * part, part), parity
+            ],
+            pot_v.at[
+                pl.ds(placed(-pot_rim, pot_rim) + pot_rim + (2 * x + o) * part, part), parity
+            ],
             pot_send.at[o], pot_recv, partners[o],
         )
         for o in range(2)
@@ -290,7 +295,15 @@
             apply(level, u + level * REACH, 1, n)
         spread(u + (DEG - 1) * REACH, n)
 
+    part_half = pot_v.at[
+        pl.ds(placed(-pot_rim, pot_rim) + pot_rim + (2 * x + core) * part, part), parity
+    ]
+    pot_pair = remote(
+        part_half, part_half, pair_send, pair_recv, {"band": band + side * (1 - 2 * parity)}
+    )
     pot_far[0].wait_recv()
+    pot_pair.start()
+    pot_pair.wait_recv()
     passed = [
         remote(mine, mine, pass_send.at[at], pass_recv.at[at], peer)
         for at, peer in enumerate(x_line)
@@ -320,6 +333,15 @@
     apply(2, slab - 20, 1)
     spread(slab - 20, 8)
     for at, (u, n) in enumerate(((0, 8), (-8, 8), (-16, 8), (-20, 4), (-24, 4))):
+        if at == 3:
+            for copy in row_copies[2]:
+                copy.wait_recv()
+            high, low = two_parts(
+                jnp.concatenate(
+                    [rows[:, :, :, k].reshape(bands, 2 * bands) for k in range(2)], axis=0
+                ).T
+            )
+            matrix[...] = jnp.concatenate([high, high, low], axis=1)
         if at == 1:
             for copy in passed:
                 copy.wait_recv()
@@ -338,10 +360,8 @@
         for o in range(2):
             far[o][5].wait_send()
 
-    for copy in (near, near_pot, *passed):
+    for copy in (near, near_pot, pot_pair, *passed):
         copy.wait_send()
-    for copy in row_copies[2]:
-        copy.wait_recv()
     for copies in row_copies:
         for copy in copies:
             copy.wait_send()
@@ -351,9 +371,8 @@
     pltpu.make_async_copy(all_but_own, all_but_own, all_recv).wait()
 
 
-def rotate_kernel(recv_v, rows_v, out, out_v, sems):
-    high, low = two_parts(jnp.concatenate([rows_v[:, 0], rows_v[:, 1]], axis=0).T)
-    matrix = jnp.concatenate([high, high, low], axis=1)
+def rotate_kernel(recv_v, matrix_v, out, out_v, sems):
+    matrix = matrix_v[...]
     width = 256
     stores = []
     for at in range(0, 8 * 128, width):
@@ -382,15 +401,16 @@
     dma = pltpu.SemaphoreType.DMA
     anywhere = pl.BlockSpec(memory_space=pl.ANY)
     slab, shift = 2 * planes, 2 * REACH
-    recv, rows = pl.pallas_call(
+    recv, matrix = pl.pallas_call(
         functools.partial(filter_kernel, bands),
         out_shape=(
             pltpu.VMEM((bands * orbs, 8, 128), f32),
-            pltpu.VMEM((4, 4, 4, orbs, 128), f32),
+            pltpu.VMEM((bands * orbs, 3 * bands * orbs), jnp.bfloat16),
         ),
         in_specs=[anywhere] * 3,
-        out_specs=(anywhere,) * 2,
+        out_specs=(anywhere, pl.BlockSpec(memory_space=pltpu.VMEM)),
         scratch_shapes=[
+            pltpu.VMEM((4, 4, 4, orbs, 128), f32),
             *[
                 pltpu.VMEM((slab + 2 * (shift + REACH * (DEG - level)), 2, 8, 128), f32)
                 for level in range(DEG)
@@ -402,6 +422,8 @@
             dma((2, 6)),
             dma((6,)),
             dma((2,)),
+            dma,
+            dma,
             dma,
             dma((7,)),
             dma((7,)),
@@ -418,7 +440,7 @@
         ),
         name="filter",
     )(*(pltpu.with_memory_space_constraint(a, pltpu.HBM) for a in (orb, pot, subspace)))
-    recv, rows = recv.reshape(bands, orbs, 8, 128), rows.reshape(bands, orbs, 128)
+    recv = recv.reshape(bands, orbs, 8, 128)
     return pl.pallas_call(
         rotate_kernel,
         out_shape=jax.ShapeDtypeStruct((bands * orbs, 1024), f32),
@@ -427,7 +449,7 @@
         scratch_shapes=[pltpu.VMEM((bands * orbs, 1024), f32), dma((4,))],
         compiler_params=pltpu.CompilerParams(vmem_limit_bytes=32 * 2**20),
         name="rotate",
-    )(*(pltpu.with_memory_space_constraint(a, pltpu.VMEM) for a in (recv, rows)))
+    )(*(pltpu.with_memory_space_constraint(a, pltpu.VMEM) for a in (recv, matrix)))
 
 
 def solution(mesh):

time: 37.2 us -> 38.5 us (1.035)
  Pallas kernels: 37.2 us -> 38.4 us
    pallas_call x1, Pallas kernels: 35.9 us -> 37.1 us  [per_device(): pl.pallas_call(functools.partial(filter_kernel, bands), out_shape=(pltpu....]
where the time goes in v10:
time: 38.5 us; the launch traced here: 38.4 us
  Pallas kernels  38.4 us (100%)
    pallas_call x1, Pallas kernels, per_device(): pl.pallas_call(functools.partial(filter_kernel, bands), out_shape=(pltpu....  37.1 us
    pallas_call x1, Pallas kernels, per_device(): pl.pallas_call(rotate_kernel, out_shape=jax.ShapeDtypeStruct((bands * orb...  1.27 us

profile of v10, /device:TPU:32, one launch (start us, length us, event | category | flops | bytes accessed | tf_op | source)
XLA Modules:
  0.0 38.4 jit_solution(5175501323724548646)
XLA Ops:
  0.0 37.1 %filter.1 = (f32[128,8,128]{2,1,0:T(8,128)S(1)}, bf16[128,384]{1,0:T(8,128)(2,1)S(1)}) custom-call(f32[2,32,2,8,128]{4,3,2,1,0:T(8,128)} %bitcast.4, f32[32,2,8,128]{3,2,1,0:T(8,128)} %bitcast.5, f32[2,128]{1,0:T(2,128)} %sub.1), custom_call_target="tpu_custom_call" | custom-call | tf_op jit(solution)/shard_map/filter/pallas_call | solution.py:404
  37.1 1.3 %rotate.1 = f32[128,1024]{1,0:T(8,128)} custom-call(f32[64,2,8,128]{3,2,1,0:T(8,128)S(1)} %bitcast.3, bf16[128,384]{1,0:T(8,128)(2,1)S(1)} %get-tuple-element.8.matrix_v), custom_call_target="tpu_custom_call" | custom-call | tf_op jit(solution)/shard_map/rotate/pallas_call | solution.py:444

commit v11 on v7

--- a/solution.py
+++ b/solution.py
@@ -85,8 +85,8 @@
 
 
 def filter_kernel(
-    bands, orb, pot, sub, recv, rows, p0, p1, p2, out, pot_v,
-    near_send, near_recv, far_send, far_recv, pot_send, pot_recv, pass_send, pass_recv,
+    bands, orb, pot, sub, recv, rows, p0, p1, p2, out, pot_v, held,
+    near_send, near_recv, far_send, far_recv, onward_send, onward_recv, pot_send, pot_recv, pass_send, pass_recv,
     move_sem, all_send, all_recv, row_send, row_recv, plane_sem, all_sem,
 ):
     quarter = orb.shape[1]
@@ -122,12 +122,15 @@
     sibling = {"dom": dom + 1 - 2 * core}
     partners = [{"dom": 2 * (1 - half) + k} for k in range(2)]
 
-    def chip_along(shift):
-        there = lax.rem(half * side + zl + shift, 2 * side)
+    def chip_along(shift, core_there=core):
+        there = lax.rem(half * side + zl + shift + 2 * side, 2 * side)
         return {
             "band": lax.rem(there, side) * floor + yx,
-            "dom": lax.div(there, side) * 2 + core,
+            "dom": lax.div(there, side) * 2 + core_there,
         }
+
+    relays = [chip_along(2 - 4 * o, o) for o in range(2)]
+    onward_to = chip_along(2 - 4 * core)
 
     x_line = [
         {"band": band - x + lax.rem(x + dx, side), "dom": dom if dk == 0 else dom + 1 - 2 * core}
@@ -139,7 +142,7 @@
     z_line = [chip_along(dz) for dz in range(1, 2 * side)]
     other_partner = {"dom": 2 * (1 - half) + 1 - core}
     barrier = pltpu.get_barrier_semaphore()
-    entered = (*z_line, other_partner, *x_line, *y_line)
+    entered = (*z_line, other_partner, chip_along(4 * core - 2, 1 - core), *x_line, *y_line)
 
     def tell(peers, semaphore):
         for peer in peers:
@@ -184,26 +187,28 @@
     gather_rows(0)
     pieces = [(0, 6), (6, 8), (14, 8), (22, 4), (26, 4)]
     assert sum(n for _, n in pieces) == rims[0]
-    far = []
-    for o in range(2):
-        group = []
-        for at, (a, n) in enumerate(pieces):
-            group.append(
+    far, onward = [[], []], []
+    for at, (a, n) in enumerate(pieces + [(slab, REACH)]):
+        if a < slab:
+            u, source = -a - n, jnp.where(left == 1, quarter - a - n, a)
+        else:
+            u, source = a, jnp.where(left == 1, 0, quarter - n)
+        slot = held.at[at, pl.ds(0, n)]
+        for o in range(2):
+            far[o].append(
                 remote(
-                    orb.at[o, pl.ds(jnp.where(left == 1, quarter - a - n, a), n)],
-                    p0.at[pl.ds(placed(-a - n, n) + rims[0], n)],
-                    far_send.at[o, at], far_recv.at[at], partners[o],
+                    orb.at[o, pl.ds(source, n)], slot,
+                    far_send.at[o, at], far_recv.at[at], relays[o],
                 )
             )
-        n = REACH
-        group.append(
+        place = jnp.where(left == 1, slab - n - u, u) + rims[0]
+        onward.append(
             remote(
-                orb.at[o, pl.ds(jnp.where(left == 1, 0, quarter - n), n)],
-                p0.at[pl.ds(placed(slab, n) + rims[0], n)],
-                far_send.at[o, 5], far_recv.at[5], partners[o],
+                slot, p0.at[pl.ds(place, n)],
+                onward_send.at[at], onward_recv.at[at], onward_to,
             )
         )
-        far.append(group)
+
     part = pot_rim // 8
     pot_far = [
         remote(
@@ -298,12 +303,19 @@
     for copy in passed:
         copy.start()
 
+    def pass_on(*numbers):
+        for at in numbers:
+            far[0][at].wait_recv()
+            onward[at].start()
+
+    pass_on(5, 0, 1)
     load.wait()
     load_pot.wait()
     own_rows.wait()
     gather_rows(1)
     near.wait_recv()
     near_pot.wait_recv()
+    pass_on(2, 3, 4)
     pl.semaphore_wait(plane_sem, len(y_line))
     tell(z_line, all_sem)
     apply(0, 8, 6)
@@ -314,7 +326,7 @@
     pl.semaphore_wait(all_sem, len(z_line))
     spread(20, 24)
 
-    far[0][5].wait_recv()
+    onward[5].wait_recv()
     apply(0, slab - 8, 1)
     apply(1, slab - 14, 1)
     apply(2, slab - 20, 1)
@@ -323,7 +335,7 @@
         if at == 1:
             for copy in passed:
                 copy.wait_recv()
-        far[0][at].wait_recv()
+        onward[at].wait_recv()
         advance(u, n)
 
     @pl.when(long)
@@ -338,7 +350,7 @@
         for o in range(2):
             far[o][5].wait_send()
 
-    for copy in (near, near_pot, *passed):
+    for copy in (near, near_pot, *onward, *passed):
         copy.wait_send()
     for copy in row_copies[2]:
         copy.wait_recv()
@@ -397,9 +409,12 @@
             ],
             pltpu.VMEM((2 * (slab + 2 * shift), 8, 128), f32),
             pltpu.VMEM((slab + 2 * (shift + REACH * (DEG - 1)), 2, 8, 128), f32),
+            pltpu.VMEM((6, 8, 2, 8, 128), f32),
             dma((2,)),
             dma((2,)),
             dma((2, 6)),
+            dma((6,)),
+            dma((6,)),
             dma((6,)),
             dma((2,)),
             dma,

time: 37.2 us -> 42.2 us (1.13)
  Pallas kernels: 37.2 us -> 42.2 us
    pallas_call x1, Pallas kernels: 35.9 us -> 40.8 us  [per_device(): pl.pallas_call(functools.partial(filter_kernel, bands), out_shape=(pltpu....]
where the time goes in v11:
time: 42.2 us
  Pallas kernels  42.2 us (100%)
    pallas_call x1, Pallas kernels, per_device(): pl.pallas_call(functools.partial(filter_kernel, bands), out_shape=(pltpu....  40.8 us
    pallas_call x1, Pallas kernels, per_device(): pl.pallas_call(rotate_kernel, out_shape=jax.ShapeDtypeStruct((bands * orb...  1.31 us

profile of v11, /device:TPU:32, one launch (start us, length us, event | category | flops | bytes accessed | tf_op | source)
XLA Modules:
  0.0 42.2 jit_solution(11976045706908776326)
XLA Ops:
  0.0 40.8 %filter.1 = (f32[128,8,128]{2,1,0:T(8,128)S(1)}, f32[4,4,4,2,128]{4,3,2,1,0:T(2,128)S(1)}) custom-call(f32[2,32,2,8,128]{4,3,2,1,0:T(8,128)} %bitcast.6, f32[32,2,8,128]{3,2,1,0:T(8,128)} %bitcast.7, f32[2,128]{1,0:T(2,128)} %sub.1), custom_call_target="tpu_custom_call" | custom-call | tf_op jit(solution)/shard_map/filter/pallas_call | solution.py:397
  40.9 1.3 %rotate.1 = f32[128,1024]{1,0:T(8,128)} custom-call(f32[64,2,8,128]{3,2,1,0:T(8,128)S(1)} %bitcast.4, f32[64,2,128]{2,1,0:T(2,128)S(1)} %bitcast.5), custom_call_target="tpu_custom_call" | custom-call | tf_op jit(solution)/shard_map/rotate/pallas_call | solution.py:437

commit v12 on v7

--- a/solution.py
+++ b/solution.py
@@ -219,9 +219,17 @@
     def _():
         for o in range(2):
             pot_far[o].start()
-        for at in range(len(pieces)):
+        for at in range(3):
             for o in range(2):
                 far[o][at].start()
+
+    def send_last():
+        for at in range(3, len(pieces)):
+            for o in range(2):
+                far[o][at].start()
+
+    inner = (zl != 0) & (zl != side - 1)
+    pl.when(long & inner)(send_last)
 
     @pl.when(jnp.logical_not(long))
     def _():
@@ -304,6 +312,7 @@
     gather_rows(1)
     near.wait_recv()
     near_pot.wait_recv()
+    pl.when(long & jnp.logical_not(inner))(send_last)
     pl.semaphore_wait(plane_sem, len(y_line))
     tell(z_line, all_sem)
     apply(0, 8, 6)

time: 37.2 us -> 37.2 us (level)
  no operation moved by 1% of the time
where the time goes in v12:
time: 37.2 us; the launch traced here: 37.1 us
  Pallas kernels  37.1 us (100%)
    pallas_call x1, Pallas kernels, per_device(): pl.pallas_call(functools.partial(filter_kernel, bands), out_shape=(pltpu....  35.8 us
    pallas_call x1, Pallas kernels, per_device(): pl.pallas_call(rotate_kernel, out_shape=jax.ShapeDtypeStruct((bands * orb...  1.31 us

profile of v12, /device:TPU:32, one launch (start us, length us, event | category | flops | bytes accessed | tf_op | source)
XLA Modules:
  0.0 37.1 jit_solution(15591873713630826453)
XLA Ops:
  0.0 35.8 %filter.1 = (f32[128,8,128]{2,1,0:T(8,128)S(1)}, f32[4,4,4,2,128]{4,3,2,1,0:T(2,128)S(1)}) custom-call(f32[2,32,2,8,128]{4,3,2,1,0:T(8,128)} %bitcast.6, f32[32,2,8,128]{3,2,1,0:T(8,128)} %bitcast.7, f32[2,128]{1,0:T(2,128)} %sub.1), custom_call_target="tpu_custom_call" | custom-call | tf_op jit(solution)/shard_map/filter/pallas_call | solution.py:394
  35.8 1.3 %rotate.1 = f32[128,1024]{1,0:T(8,128)} custom-call(f32[64,2,8,128]{3,2,1,0:T(8,128)S(1)} %bitcast.4, f32[64,2,128]{2,1,0:T(2,128)S(1)} %bitcast.5), custom_call_target="tpu_custom_call" | custom-call | tf_op jit(solution)/shard_map/rotate/pallas_call | solution.py:431

commit v13 on v8

--- a/solution.py
+++ b/solution.py
@@ -307,11 +307,17 @@
     load_pot.wait()
     own_rows.wait()
     gather_rows(1)
+
+    def two_blocks(first):
+        apply(0, jnp.where(left == 1, first, slab - 16 - first), 2)
+
+    two_blocks(core * quarter + 8)
     near.wait_recv()
     near_pot.wait_recv()
     pl.semaphore_wait(plane_sem, len(y_line))
     tell(z_line, all_sem)
-    apply(0, 8, 6)
+    two_blocks((1 - core) * quarter + 8)
+    apply(0, 24, 2)
     apply(1, 14, 4)
     apply(1, 42, 1)
     apply(2, 20, 3)

time: 38.1 us -> 38.1 us (level)
  no operation moved by 1% of the time
where the time goes in v13:
time: 38.1 us; the launch traced here: 38 us
  Pallas kernels  38 us (100%)
    pallas_call x1, Pallas kernels, per_device(): pl.pallas_call(functools.partial(filter_kernel, bands), out_shape=(pltpu....  36.7 us
    pallas_call x1, Pallas kernels, per_device(): pl.pallas_call(rotate_kernel, out_shape=jax.ShapeDtypeStruct((bands * orb...  1.31 us

profile of v13, /device:TPU:32, one launch (start us, length us, event | category | flops | bytes accessed | tf_op | source)
XLA Modules:
  0.0 38.0 jit_solution(8731964771560952660)
XLA Ops:
  0.0 36.7 %filter.1 = (f32[128,8,128]{2,1,0:T(8,128)S(1)}, f32[4,4,4,2,128]{4,3,2,1,0:T(2,128)S(1)}) custom-call(f32[2,32,2,8,128]{4,3,2,1,0:T(8,128)} %bitcast.6, f32[32,2,8,128]{3,2,1,0:T(8,128)} %bitcast.7, f32[2,128]{1,0:T(2,128)} %sub.1), custom_call_target="tpu_custom_call" | custom-call | tf_op jit(solution)/shard_map/filter/pallas_call | solution.py:396
  36.7 1.3 %rotate.1 = f32[128,1024]{1,0:T(8,128)} custom-call(f32[64,2,8,128]{3,2,1,0:T(8,128)S(1)} %bitcast.4, f32[64,2,128]{2,1,0:T(2,128)S(1)} %bitcast.5), custom_call_target="tpu_custom_call" | custom-call | tf_op jit(solution)/shard_map/rotate/pallas_call | solution.py:433

commit v14 on v12

--- a/solution.py
+++ b/solution.py
@@ -267,7 +267,7 @@
                 out[pl.ds(2 * (at + rims[DEG]), 2 * step)] = pairs.reshape(2 * step, 8, 128)
             return c
 
-        lax.fori_loop(0, blocks, body, 0)
+        lax.fori_loop(0, blocks, body, 0, unroll=min(blocks, 3))
 
     row = 2 * band + core
 
@@ -310,12 +310,18 @@
     load_pot.wait()
     own_rows.wait()
     gather_rows(1)
+
+    def two_blocks(first):
+        apply(0, jnp.where(left == 1, first, slab - 16 - first), 2)
+
+    two_blocks(core * quarter + 8)
     near.wait_recv()
     near_pot.wait_recv()
     pl.when(long & jnp.logical_not(inner))(send_last)
     pl.semaphore_wait(plane_sem, len(y_line))
     tell(z_line, all_sem)
-    apply(0, 8, 6)
+    two_blocks((1 - core) * quarter + 8)
+    apply(0, 24, 2)
     apply(1, 14, 4)
     apply(1, 42, 1)
     apply(2, 20, 3)

time: 37.2 us -> 37.7 us (1.013)
  Pallas kernels: 37.1 us -> 37.6 us
    pallas_call x1, Pallas kernels: 35.8 us -> 36.3 us  [per_device(): pl.pallas_call(functools.partial(filter_kernel, bands), out_shape=(pltpu....]
where the time goes in v14:
time: 37.7 us; the launch traced here: 37.6 us
  Pallas kernels  37.6 us (100%)
    pallas_call x1, Pallas kernels, per_device(): pl.pallas_call(functools.partial(filter_kernel, bands), out_shape=(pltpu....  36.3 us
    pallas_call x1, Pallas kernels, per_device(): pl.pallas_call(rotate_kernel, out_shape=jax.ShapeDtypeStruct((bands * orb...  1.31 us

profile of v14, /device:TPU:32, one launch (start us, length us, event | category | flops | bytes accessed | tf_op | source)
XLA Modules:
  0.0 37.6 jit_solution(2468706149298637634)
XLA Ops:
  0.0 36.3 %filter.1 = (f32[128,8,128]{2,1,0:T(8,128)S(1)}, f32[4,4,4,2,128]{4,3,2,1,0:T(2,128)S(1)}) custom-call(f32[2,32,2,8,128]{4,3,2,1,0:T(8,128)} %bitcast.6, f32[32,2,8,128]{3,2,1,0:T(8,128)} %bitcast.7, f32[2,128]{1,0:T(2,128)} %sub.1), custom_call_target="tpu_custom_call" | custom-call | tf_op jit(solution)/shard_map/filter/pallas_call | solution.py:400
  36.3 1.3 %rotate.1 = f32[128,1024]{1,0:T(8,128)} custom-call(f32[64,2,8,128]{3,2,1,0:T(8,128)S(1)} %bitcast.4, f32[64,2,128]{2,1,0:T(2,128)S(1)} %bitcast.5), custom_call_target="tpu_custom_call" | custom-call | tf_op jit(solution)/shard_map/rotate/pallas_call | solution.py:437

commit v15 on v12

--- a/solution.py
+++ b/solution.py
@@ -276,7 +276,7 @@
         tiles = 2 * count
 
         def send(i, c):
-            at = lax.rem(i + yx * max(tiles // floor, 1), tiles)
+            at = lax.rem(i + yx * max(tiles // floor, 1) + 4 * zl + 2 * core, tiles)
             tile = lax.rem(2 * (base + start) + at + 2 * whole, 2 * whole)
             src = out.at[2 * (start + rims[DEG]) + at]
 

time: 37.2 us -> 37.2 us (level)
  no operation moved by 1% of the time
where the time goes in v15:
time: 37.2 us; the launch traced here: 37.1 us
  Pallas kernels  37.1 us (100%)
    pallas_call x1, Pallas kernels, per_device(): pl.pallas_call(functools.partial(filter_kernel, bands), out_shape=(pltpu....  35.8 us
    pallas_call x1, Pallas kernels, per_device(): pl.pallas_call(rotate_kernel, out_shape=jax.ShapeDtypeStruct((bands * orb...  1.31 us

profile of v15, /device:TPU:32, one launch (start us, length us, event | category | flops | bytes accessed | tf_op | source)
XLA Modules:
  0.0 37.1 jit_solution(13441052362882267575)
XLA Ops:
  0.0 35.8 %filter.1 = (f32[128,8,128]{2,1,0:T(8,128)S(1)}, f32[4,4,4,2,128]{4,3,2,1,0:T(2,128)S(1)}) custom-call(f32[2,32,2,8,128]{4,3,2,1,0:T(8,128)} %bitcast.6, f32[32,2,8,128]{3,2,1,0:T(8,128)} %bitcast.7, f32[2,128]{1,0:T(2,128)} %sub.1), custom_call_target="tpu_custom_call" | custom-call | tf_op jit(solution)/shard_map/filter/pallas_call | solution.py:394
  35.8 1.3 %rotate.1 = f32[128,1024]{1,0:T(8,128)} custom-call(f32[64,2,8,128]{3,2,1,0:T(8,128)S(1)} %bitcast.4, f32[64,2,128]{2,1,0:T(2,128)S(1)} %bitcast.5), custom_call_target="tpu_custom_call" | custom-call | tf_op jit(solution)/shard_map/rotate/pallas_call | solution.py:431

commit v16 on v15

--- a/solution.py
+++ b/solution.py
@@ -271,7 +271,7 @@
 
     row = 2 * band + core
 
-    def spread(u, count):
+    def spread(u, count, first=0, last=None):
         start = placed(u, count)
         tiles = 2 * count
 
@@ -291,7 +291,7 @@
 
             return c
 
-        lax.fori_loop(0, tiles, send, 0)
+        lax.fori_loop(first, tiles if last is None else last, send, 0)
 
     def advance(u, n):
         for level in range(DEG):
@@ -321,7 +321,7 @@
     apply(2, 20, 3)
     gather_rows(2)
     pl.semaphore_wait(all_sem, len(z_line))
-    spread(20, 24)
+    spread(20, 24, 0, 24)
 
     far[0][5].wait_recv()
     apply(0, slab - 8, 1)
@@ -334,6 +334,8 @@
                 copy.wait_recv()
         far[0][at].wait_recv()
         advance(u, n)
+        if at == 2:
+            spread(20, 24, 24, 48)
 
     @pl.when(long)
     def _():

time: 37.2 us -> 39.1 us (1.051)
  Pallas kernels: 37.1 us -> 39.1 us
    pallas_call x1, Pallas kernels: 35.8 us -> 37.7 us  [per_device(): pl.pallas_call(functools.partial(filter_kernel, bands), out_shape=(pltpu....]
where the time goes in v16:
time: 39.1 us
  Pallas kernels  39.1 us (100%)
    pallas_call x1, Pallas kernels, per_device(): pl.pallas_call(functools.partial(filter_kernel, bands), out_shape=(pltpu....  37.7 us
    pallas_call x1, Pallas kernels, per_device(): pl.pallas_call(rotate_kernel, out_shape=jax.ShapeDtypeStruct((bands * orb...  1.31 us

profile of v16, /device:TPU:32, one launch (start us, length us, event | category | flops | bytes accessed | tf_op | source)
XLA Modules:
  0.0 39.1 jit_solution(1361765513546022547)
XLA Ops:
  0.0 37.7 %filter.1 = (f32[128,8,128]{2,1,0:T(8,128)S(1)}, f32[4,4,4,2,128]{4,3,2,1,0:T(2,128)S(1)}) custom-call(f32[2,32,2,8,128]{4,3,2,1,0:T(8,128)} %bitcast.6, f32[32,2,8,128]{3,2,1,0:T(8,128)} %bitcast.7, f32[2,128]{1,0:T(2,128)} %sub.1), custom_call_target="tpu_custom_call" | custom-call | tf_op jit(solution)/shard_map/filter/pallas_call | solution.py:396
  37.8 1.3 %rotate.1 = f32[128,1024]{1,0:T(8,128)} custom-call(f32[64,2,8,128]{3,2,1,0:T(8,128)S(1)} %bitcast.4, f32[64,2,128]{2,1,0:T(2,128)S(1)} %bitcast.5), custom_call_target="tpu_custom_call" | custom-call | tf_op jit(solution)/shard_map/rotate/pallas_call | solution.py:433

commit v17 on v14

--- a/solution.py
+++ b/solution.py
@@ -276,7 +276,7 @@
         tiles = 2 * count
 
         def send(i, c):
-            at = lax.rem(i + yx * max(tiles // floor, 1), tiles)
+            at = lax.rem(i + yx * max(tiles // floor, 1) + 4 * zl + 2 * core, tiles)
             tile = lax.rem(2 * (base + start) + at + 2 * whole, 2 * whole)
             src = out.at[2 * (start + rims[DEG]) + at]
 

time: 37.7 us -> 37.6 us (level)
  no operation moved by 1% of the time
where the time goes in v17:
time: 37.6 us
  Pallas kernels  37.5 us (100%)
    pallas_call x1, Pallas kernels, per_device(): pl.pallas_call(functools.partial(filter_kernel, bands), out_shape=(pltpu....  36.2 us
    pallas_call x1, Pallas kernels, per_device(): pl.pallas_call(rotate_kernel, out_shape=jax.ShapeDtypeStruct((bands * orb...  1.31 us

profile of v17, /device:TPU:32, one launch (start us, length us, event | category | flops | bytes accessed | tf_op | source)
XLA Modules:
  0.0 37.6 jit_solution(2216803368784927729)
XLA Ops:
  0.0 36.2 %filter.1 = (f32[128,8,128]{2,1,0:T(8,128)S(1)}, f32[4,4,4,2,128]{4,3,2,1,0:T(2,128)S(1)}) custom-call(f32[2,32,2,8,128]{4,3,2,1,0:T(8,128)} %bitcast.6, f32[32,2,8,128]{3,2,1,0:T(8,128)} %bitcast.7, f32[2,128]{1,0:T(2,128)} %sub.1), custom_call_target="tpu_custom_call" | custom-call | tf_op jit(solution)/shard_map/filter/pallas_call | solution.py:400
  36.2 1.3 %rotate.1 = f32[128,1024]{1,0:T(8,128)} custom-call(f32[64,2,8,128]{3,2,1,0:T(8,128)S(1)} %bitcast.4, f32[64,2,128]{2,1,0:T(2,128)S(1)} %bitcast.5), custom_call_target="tpu_custom_call" | custom-call | tf_op jit(solution)/shard_map/rotate/pallas_call | solution.py:437
